TPU v7x, 32 devices: a whole 2x2x4 slice. The times are simulated.
32 devices in a mesh: lat: 4 (over y, core), lon: 4 (over z), ens: 2 (over x).
Axes of the slice: x: 2, y: 2, z: 4, core: 2. Of those that a mesh axis runs over, the one named last changes fastest.
Arguments:
- fields: bfloat16 [2, 48, 64, 640], P('ens', 'lat', 'lon'), may hold values from -6 to 6
- filter_basis: bfloat16 [48, 5, 4, 16], P(('lat', 'lon')), may hold values from -0.625 to 0.625
- lon_offsets: int32 [48, 5, 16], P(('lat', 'lon')), may hold values from -32 to 31, as said below
- conv_weight: bfloat16 [2560, 640], replicated, may hold values from -0.125 to 0.125
- weight_in: bfloat16 [640, 1280], replicated, may hold values from -0.25 to 0.25
- weight_out: bfloat16 [1280, 640], replicated, may hold values from -0.15625 to 0.15625
- cotangent: bfloat16 [2, 48, 64, 640], P('ens', 'lat', 'lon'), may hold values from -6 to 6
Outputs:
- block_out: bfloat16 [2, 48, 64, 640], P('ens', 'lat', 'lon')
- field_grad: bfloat16 [2, 48, 64, 640], P('ens', 'lat', 'lon')
- conv_weight_grad: float32 [2560, 640], P(('lat', 'lon', 'ens'))
- weight_in_grad: float32 [640, 1280], P(None, ('lat', 'lon', 'ens'))
- weight_out_grad: float32 [1280, 640], P(('lat', 'lon', 'ens'))
Inputs may be any that keep to these rules, and one draw needn't show every extreme that they name: `lon_offsets`: within one cycle and one cycle offset the 16 longitude offsets are distinct. In the 2 cycles nearest each pole they lie in -32 to 31; in every other cycle they lie in -16 to 15.
All inputs are finite; a program needn't handle non-finite values.
Results may differ from a plain program's by a relative error of at most 0.015.
Values may be sent and summed in bfloat16 or wider, within the bound.
A program may use at most 128 MiB of HBM per device.

v0:
```python
import functools
import math

import jax
import jax.numpy as jnp
from jax import lax
from jax.experimental import pallas as pl
from jax.experimental.pallas import tpu as pltpu
from jax.sharding import PartitionSpec as P

HALF_ROOT = 0.7071067811865476
GAUSS_NORM = 0.3989422804014327
MESH = pl.DeviceIdType.MESH
F32 = jnp.float32
BF16 = jnp.bfloat16


def mm(left, right, contract):
    return lax.dot_general(left, right, ((contract[:1], contract[1:]), ((), ())),
                           preferred_element_type=F32)


class Plan:
    def __init__(self, fields, filter_basis, weight_in):
        self.lat, self.lon = lax.axis_size("lat"), lax.axis_size("lon")
        self.ens = lax.axis_size("ens")
        _, self.tile, self.width, self.embed = fields.shape
        self.band, self.span, self.basis, self.taps = filter_basis.shape
        self.hidden = weight_in.shape[1]
        self.reach = self.span // 2
        self.nlon = self.lon * self.width
        self.cells = self.band * self.nlon
        self.cores = 2 if self.lat % 2 == 0 else 1
        self.rows = self.lat // self.cores
        self.members = 1
        for members in (self.ens, 1):
            blocks = self.lat * self.lon * members
            conv_rows = self.basis * self.embed // blocks
            in_rows = self.hidden // blocks
            if conv_rows % 16 == 0 and in_rows % 8 == 0 and self.embed % conv_rows == 0:
                self.members = members
                break
        self.blocks = self.lat * self.lon * self.members
        self.conv_rows = self.basis * self.embed // self.blocks
        self.in_rows = self.hidden // self.blocks
        self.half = self.blocks // self.cores
        width = 256
        self.groups = [(c, min(width, self.embed - c)) for c in range(0, self.embed, width)]


def kernel(
    g, basis_hbm, offsets_hbm, fields, cot, conv_hbm, in_hbm, out_hbm,
    block_out, field_grad, conv_out, io_out,
    basis_ref, offsets_ref, taps_ref, conv_w, w_in, w_out, win, cot_band, matrix, spread, blended, hidden, pgrad, bgrad,
    sgrad, adj, bo_band, fg_band, rim_send, rim_recv,
    conv_g, io_g, conv_c, io_c, conv_s0, io_s0, conv_r1, io_r1, conv_s1, io_s1,
    conv_r2, io_r2, conv_s2, io_s2, conv_r3, io_r3,
    local_sem, gather_send, gather_recv, edge_sem, cot_send, cot_recv,
    bo_send, bo_recv, fg_send, fg_recv, rim_ssem, rim_rsem,
    core_send, core_recv, st_send, st_recv, lon_send, lon_recv,
):
    a, j, e = lax.axis_index("lat"), lax.axis_index("lon"), lax.axis_index("ens")
    L, s, W, T, C = g.lon, g.band, g.width, g.tile, g.embed
    rr = g.reach
    core, y = lax.rem(a, g.cores), lax.div(a, g.cores)
    b = a * L + j
    last = g.lat * L - 1

    def remote(src, dst, ssem, rsem, **device):
        return pltpu.make_async_remote_copy(
            src_ref=src, dst_ref=dst, send_sem=ssem, recv_sem=rsem,
            device_id=device, device_id_type=MESH)

    def columns(index):
        return pl.ds(pl.multiple_of(index * W, W), W)

    weights = [
        pltpu.make_async_copy(src, dst, local_sem.at[i])
        for i, (src, dst) in enumerate(((conv_hbm, conv_w), (in_hbm, w_in), (out_hbm, w_out)))
    ]
    own_field = pltpu.make_async_copy(
        fields.at[0, pl.ds(j * s, s)], win.at[pl.ds(rr, s), columns(j)], local_sem.at[3])
    own_cot = pltpu.make_async_copy(
        cot.at[0, pl.ds(j * s, s)], cot_band.at[:, columns(j)], local_sem.at[4])
    basis_copy = pltpu.make_async_copy(basis_hbm, basis_ref, local_sem.at[5])
    offsets_copy = pltpu.make_async_copy(offsets_hbm, offsets_ref, local_sem.at[6])
    basis_copy.start()
    offsets_copy.start()
    own_field.start()
    own_cot.start()

    barrier = pltpu.get_barrier_semaphore()
    count = 0
    for step in (1, g.lat - 1):
        for q in range(L):
            pl.semaphore_signal(barrier, inc=1, device_id_type=MESH,
                                device_id={"lat": lax.rem(a + step, g.lat), "lon": q})
            count += 1
    for d in range(1, L):
        pl.semaphore_signal(barrier, inc=1, device_id_type=MESH,
                            device_id={"lon": lax.rem(j + d, L)})
        count += 1
    for d in range(1, g.rows):
        pl.semaphore_signal(barrier, inc=1, device_id_type=MESH,
                            device_id={"lat": lax.rem(y + d, g.rows) * g.cores + core})
        count += 1
    for d in range(1, g.members):
        pl.semaphore_signal(barrier, inc=1, device_id_type=MESH,
                            device_id={"ens": lax.rem(e + d, g.members)})
        count += 1
    pl.semaphore_wait(barrier, count)

    def low_src(p):
        return fields.at[0, pl.ds(lax.rem(p * s - rr + T, T), rr)]

    def high_src(p):
        return fields.at[0, pl.ds(lax.rem(p * s + s, T), rr)]

    low_rows, mid_rows, high_rows = pl.ds(0, rr), pl.ds(rr, s), pl.ds(rr + s, rr)

    def up(p):
        return lax.rem(a + (p == 0).astype(jnp.int32), g.lat)

    def down(p):
        return lax.rem(a + g.lat - (p == L - 1).astype(jnp.int32), g.lat)

    sends = []
    for d in range(1, L):
        p = lax.rem(j + d, L)
        triple = (
            (fields.at[0, pl.ds(p * s, s)], mid_rows, a),
            (low_src(p), low_rows, up(p)),
            (high_src(p), high_rows, down(p)),
        )
        for i, (src, rows, row) in enumerate(triple):
            copy = remote(src, win.at[rows, columns(j)], gather_send.at[d - 1, i],
                          gather_recv.at[d - 1, i], lat=row, lon=p)
            copy.start()
            sends.append(copy)
    low_local = pltpu.make_async_copy(low_src(j), win.at[low_rows, columns(j)], edge_sem.at[0])
    low_remote = remote(low_src(j), win.at[low_rows, columns(j)], edge_sem.at[2],
                        edge_sem.at[0], lat=lax.rem(a + 1, g.lat))
    high_local = pltpu.make_async_copy(high_src(j), win.at[high_rows, columns(j)], edge_sem.at[1])
    high_remote = remote(high_src(j), win.at[high_rows, columns(j)], edge_sem.at[3],
                         edge_sem.at[1], lat=lax.rem(a + g.lat - 1, g.lat))

    @pl.when(j == 0)
    def _():
        low_remote.start()

    @pl.when(j != 0)
    def _():
        low_local.start()

    @pl.when(j == L - 1)
    def _():
        high_remote.start()

    @pl.when(j != L - 1)
    def _():
        high_local.start()

    for copy in weights:
        copy.start()

    NL, K, TAPS = g.nlon, g.basis, g.taps
    wide = g.span * NL
    step_rows = 16
    steps = NL // step_rows
    places = lax.broadcasted_iota(jnp.int32, (step_rows, wide), 1)
    lines = lax.broadcasted_iota(jnp.int32, (step_rows, wide), 0)

    def build(i, _):
        r, n0 = lax.div(i, steps), lax.rem(i, steps) * step_rows
        gap = lax.rem(lax.rem(places, NL) - lines - n0 + (NL + NL // 2), NL) - NL // 2
        gap = gap.astype(F32)
        sums = [jnp.zeros((step_rows, wide), F32) for _ in range(K)]
        for t in range(TAPS):
            hit = gap == taps_ref[r, pl.ds(t, 1), :]
            for k in range(K):
                value = taps_ref[r, pl.ds(TAPS * (k + 1) + t, 1), :]
                sums[k] = jnp.where(hit, value, sums[k])
        for k in range(K):
            start = pl.multiple_of(k * NL + n0, step_rows)
            matrix[r, pl.ds(start, step_rows), :] = sums[k].astype(BF16)
        return 0

    ones = (lax.broadcasted_iota(jnp.int32, (g.span, wide), 1) // NL
            == lax.broadcasted_iota(jnp.int32, (g.span, wide), 0)).astype(BF16)
    basis_copy.wait()
    offsets_copy.wait()
    for r in range(s):
        taps_ref[r, 0:TAPS] = mm(offsets_ref[:, r, :].astype(F32).astype(BF16), ones, (0, 0))
        for k in range(K):
            taps_ref[r, TAPS * (k + 1):TAPS * (k + 2)] = mm(basis_ref[r, :, k, :], ones, (0, 0))
    lax.fori_loop(0, s * steps, build, 0)

    own_field.wait()
    for d in range(1, L):
        source = lax.rem(j - d + L, L)
        for i, rows in enumerate((mid_rows, low_rows, high_rows)):
            landed = win.at[rows, columns(source)]
            remote(landed, landed, gather_send.at[d - 1, i], gather_recv.at[d - 1, i],
                   lon=source).wait_recv()

    @pl.when(j == 0)
    def _():
        low_remote.wait()

    @pl.when(j != 0)
    def _():
        low_local.wait()

    @pl.when(j == L - 1)
    def _():
        high_remote.wait()

    @pl.when(j != L - 1)
    def _():
        high_local.wait()

    for d in range(1, L):
        p = lax.rem(j + d, L)
        copy = remote(cot.at[0, pl.ds(p * s, s)], cot_band.at[:, columns(j)],
                      cot_send.at[d - 1], cot_recv.at[d - 1], lon=p)
        copy.start()
        sends.append(copy)

    @pl.when(b == 0)
    def _():
        win[0:rr] = jnp.zeros((rr, NL, C), BF16)

    @pl.when(b == last)
    def _():
        win[rr + s:] = jnp.zeros((rr, NL, C), BF16)

    for r in range(s):
        window = win[r:r + g.span].reshape(wide, C)
        part = mm(matrix[r], window, (1, 0)).astype(BF16)
        for k in range(K):
            spread[r * NL:(r + 1) * NL, k * C:(k + 1) * C] = part[k * NL:(k + 1) * NL]
    weights[0].wait()
    blended[...] = (
        win[rr:rr + s].reshape(g.cells, C).astype(F32) + mm(spread[...], conv_w[...], (1, 0))
    ).astype(BF16)

    own_cot.wait()
    for d in range(1, L):
        source = lax.rem(j - d + L, L)
        landed = cot_band.at[:, columns(source)]
        remote(landed, landed, cot_send.at[d - 1], cot_recv.at[d - 1], lon=source).wait_recv()
    weights[1].wait()
    weights[2].wait()
    lanes = 256 if g.hidden % 256 == 0 else g.hidden

    def units(i, _):
        cols = pl.ds(pl.multiple_of(i * lanes, lanes), lanes)
        pre = mm(blended[...], w_in[:, cols], (1, 0))
        cdf = 0.5 * (1.0 + lax.erf(pre * HALF_ROOT))
        hidden[:, cols] = (pre * cdf).astype(BF16)
        hgrad = mm(cot_band[...].reshape(g.cells, C), w_out[cols, :], (1, 1))
        slope = cdf + pre * jnp.exp(-0.5 * pre * pre) * GAUSS_NORM
        pgrad[:, cols] = (hgrad * slope).astype(BF16)
        return 0

    lax.fori_loop(0, g.hidden // lanes, units, 0)

    def send_tiles(band, out, ssem, rsem):
        copies = []
        for d in range(1, L):
            p = lax.rem(j + d, L)
            copy = remote(band.at[:, columns(p)], out.at[0, pl.ds(j * s, s)],
                          ssem.at[d - 1], rsem.at[d - 1], lon=p)
            copy.start()
            copies.append(copy)
        out[0, pl.ds(j * s, s)] = band[:, columns(j), :]
        return copies

    def await_tiles(out, ssem, rsem):
        for d in range(1, L):
            source = lax.rem(j - d + L, L)
            landed = out.at[0, pl.ds(source * s, s)]
            remote(landed, landed, ssem.at[d - 1], rsem.at[d - 1], lon=source).wait_recv()

    E, Y, half = g.members, g.rows, g.half
    ri, rc = g.in_rows, g.conv_rows
    groups = range(len(g.groups))

    def place(index, order):
        member = lax.rem(index, E)
        column = lax.rem(lax.div(index, E), L)
        row = lax.div(index, E * L)
        row_core, row_y = lax.rem(row, g.cores), lax.div(row, g.cores)
        outer = member * Y + row_y if order == "ens" else row_y * E + member
        return row_core, outer * L + column

    def cut(h):
        return pl.ds(*g.groups[h])

    def add(blocks):
        if len(blocks) == 2:
            return blocks[0] + blocks[1]
        return sum((block.astype(F32) for block in blocks[1:]), blocks[0].astype(F32)).astype(BF16)

    def io_blocks(i, _):
        cols = pl.ds(pl.multiple_of(i * C, 128), C)
        left = mm(pgrad[:, cols], blended[...], (0, 0))
        right = mm(hidden[:, cols], cot_band[...].reshape(g.cells, C), (0, 0))
        for c in range(C // ri):
            where, flat = place(i * (C // ri) + c, "ens")
            both = jnp.concatenate([left[c * ri:(c + 1) * ri], right[c * ri:(c + 1) * ri]], 0)
            io_g[where, flat] = both.astype(BF16)
        return 0

    def conv_blocks(i, _):
        cols = pl.ds(pl.multiple_of(i * C, 128), C)
        product = mm(spread[:, cols], bgrad[...], (0, 0))
        for c in range(C // rc):
            where, flat = place(i * (C // rc) + c, "lat")
            conv_g[where, flat] = product[c * rc:(c + 1) * rc].astype(BF16)
        return 0

    def core_copies(src, dst, index):
        return [
            remote(src.at[1 - core, :, :, cut(h)], dst.at[:, :, cut(h)],
                   core_send.at[index, h], core_recv.at[index, h],
                   lat=y * g.cores + 1 - core)
            for h in groups
        ]

    def core_sum(total, own, other, h):
        def one(i, _):
            blocks = [own[core, i, :, cut(h)]]
            if g.cores > 1:
                blocks.append(other[i, :, cut(h)])
            total[i, :, cut(h)] = add(blocks)
            return 0
        lax.fori_loop(0, half, one, 0)

    def stage(axis):
        if axis == "ens":
            return E, e, [({"ens": lax.rem(e + d, E)}, lax.rem(e + d, E)) for d in range(1, E)]
        turns = [lax.rem(y + d, Y) for d in range(1, Y)]
        return Y, y, [({"lat": p * g.cores + core}, p) for p in turns]

    def stage_start(axis, src, dst, h, sem_row):
        _, _, peers = stage(axis)
        m = dst.shape[1]
        copies = []
        for d, (device, p) in enumerate(peers):
            copy = remote(src.at[pl.ds(p * m, m), :, cut(h)], dst.at[d, :, :, cut(h)],
                          st_send.at[sem_row, h, d], st_recv.at[sem_row, h, d], **device)
            copy.start()
            copies.append(copy)
        return copies

    def stage_sum(axis, src, dst, total, h):
        n, me, _ = stage(axis)
        m = dst.shape[1]

        def one(i, _):
            total[i, :, cut(h)] = add(
                [src[me * m + i, :, cut(h)]] + [dst[d, i, :, cut(h)] for d in range(n - 1)])
            return 0

        lax.fori_loop(0, m, one, 0)

    def lon_start(src, dst, h, sem_row):
        copies = []
        for d in range(1, L):
            p = lax.rem(j + d, L)
            copy = remote(src.at[p, :, cut(h)], dst.at[d - 1, :, cut(h)],
                          lon_send.at[sem_row, h, d - 1], lon_recv.at[sem_row, h, d - 1], lon=p)
            copy.start()
            copies.append(copy)
        return copies

    def lon_sum(src, dst, total, h, copies):
        block = src[j, :, cut(h)].astype(F32)
        for d, copy in enumerate(copies):
            copy.wait()
            block = block + dst[d, :, cut(h)].astype(F32)
        total[:, cut(h)] = block

    lax.fori_loop(0, g.hidden // C, io_blocks, 0)
    io_core = core_copies(io_g, io_c, 0)
    conv_core = core_copies(conv_g, conv_c, 1)
    if g.cores > 1:
        io_core[0].start()
    bgrad[...] = (
        cot_band[...].reshape(g.cells, C).astype(F32) + mm(pgrad[...], w_in[...], (1, 1))
    ).astype(BF16)
    io_1, conv_1, io_2, conv_2, io_3, conv_3 = ([None for _ in groups] for _ in range(6))

    def after_core(copies, total, own, other, h):
        if g.cores > 1:
            copies[h].wait()
        core_sum(total, own, other, h)

    def start_rest(copies):
        if g.cores > 1:
            for copy in copies[1:]:
                copy.start()

    def finish_stage(copies):
        for copy in copies:
            copy.wait()

    start_rest(io_core)
    after_core(io_core, io_s0, io_g, io_c, 0)
    io_1[0] = stage_start("ens", io_s0, io_r1, 0, 0)
    lax.fori_loop(0, K, conv_blocks, 0)
    if g.cores > 1:
        conv_core[0].start()
    bo_band[...] = (
        blended[...].astype(F32) + mm(hidden[...], w_out[...], (1, 0))
    ).astype(BF16).reshape(s, NL, C)
    sends += send_tiles(bo_band, block_out, bo_send, bo_recv)
    start_rest(conv_core)
    after_core(conv_core, conv_s0, conv_g, conv_c, 0)
    conv_1[0] = stage_start("lat", conv_s0, conv_r1, 0, 1)

    sgrad[...] = mm(bgrad[...], conv_w[...], (1, 1)).astype(BF16)
    for r in range(s):
        grad = jnp.concatenate(
            [sgrad[r * NL:(r + 1) * NL, k * C:(k + 1) * C] for k in range(K)], 0)
        part = mm(matrix[r], grad, (0, 0)).reshape(g.span, NL, C)
        if r == 0:
            adj[0:g.span] = part
            adj[g.span:] = jnp.zeros((s - 1, NL, C), F32)
        else:
            adj[r:r + g.span] += part

    rim_send[0] = adj[0:rr].astype(BF16)
    rim_send[1] = adj[rr + s:].astype(BF16)
    before = lax.rem(b + last, last + 1)
    after = lax.rem(b + 1, last + 1)
    rims = [
        remote(rim_send.at[0], rim_recv.at[0], rim_ssem.at[0], rim_rsem.at[0],
               lat=lax.div(before, L), lon=lax.rem(before, L)),
        remote(rim_send.at[1], rim_recv.at[1], rim_ssem.at[1], rim_rsem.at[1],
               lat=lax.div(after, L), lon=lax.rem(after, L)),
    ]
    for copy in rims:
        copy.start()

    def return_fields():
        for copy in rims:
            copy.wait()
        from_next = jnp.where(b == last, 0.0, rim_recv[0].astype(F32))
        from_prev = jnp.where(b == 0, 0.0, rim_recv[1].astype(F32))
        adj[rr:2 * rr] += from_prev
        adj[s:s + rr] += from_next
        fg_band[...] = (
            bgrad[...].astype(F32).reshape(s, NL, C) + adj[rr:rr + s]
        ).astype(BF16)
        return send_tiles(fg_band, field_grad, fg_send, fg_recv)

    for h in groups:
        more = h + 1 < len(groups)
        if more:
            after_core(io_core, io_s0, io_g, io_c, h + 1)
            after_core(conv_core, conv_s0, conv_g, conv_c, h + 1)
        finish_stage(io_1[h])
        if more:
            io_1[h + 1] = stage_start("ens", io_s0, io_r1, h + 1, 0)
        stage_sum("ens", io_s0, io_r1, io_s1, h)
        io_2[h] = stage_start("lat", io_s1, io_r2, h, 2)
        finish_stage(conv_1[h])
        if more:
            conv_1[h + 1] = stage_start("lat", conv_s0, conv_r1, h + 1, 1)
        stage_sum("lat", conv_s0, conv_r1, conv_s1, h)
        conv_2[h] = stage_start("ens", conv_s1, conv_r2, h, 3)
        if h == 0:
            sends += return_fields()
        finish_stage(io_2[h])
        stage_sum("lat", io_s1, io_r2, io_s2, h)
        io_3[h] = lon_start(io_s2, io_r3, h, 0)
        finish_stage(conv_2[h])
        stage_sum("ens", conv_s1, conv_r2, conv_s2, h)
        conv_3[h] = lon_start(conv_s2, conv_r3, h, 1)
    await_tiles(block_out, bo_send, bo_recv)
    await_tiles(field_grad, fg_send, fg_recv)
    for h in groups:
        lon_sum(io_s2, io_r3, io_out, h, io_3[h])
        lon_sum(conv_s2, conv_r3, conv_out, h, conv_3[h])
    for copy in sends:
        copy.wait_send()


def finish(rows, factor, bo, fg, conv, io, block_out, field_grad, conv_grad, in_grad, out_grad):
    block_out[...] = bo[...]
    field_grad[...] = fg[...]
    conv_grad[...] = conv[...] * factor
    in_grad[...] = io[:rows] * factor
    out_grad[...] = io[rows:] * factor


def shards(fields, filter_basis, lon_offsets, conv_weight, weight_in, weight_out, cotangent):
    g = Plan(fields, filter_basis, weight_in)
    C, H, K, L, s = g.embed, g.hidden, g.basis, g.lon, g.band
    vmem, dma = pltpu.VMEM, pltpu.SemaphoreType.DMA
    rc, rio, half = g.conv_rows, 2 * g.in_rows, g.half
    peers = max(g.rows, g.members, 2) - 1

    def slots(n):
        return max(n - 1, 1)

    cuts = len(g.groups)
    after_ens, after_lat = half // g.members, half // g.rows
    scratch = [
        vmem(filter_basis.shape, BF16), vmem((g.span, s, g.taps), jnp.int32),
        vmem((s, (K + 1) * g.taps, g.span * g.nlon), F32), vmem((K * C, C), BF16), vmem((C, H), BF16), vmem((H, C), BF16),
        vmem((s + 2 * g.reach, g.nlon, C), BF16), vmem((s, g.nlon, C), BF16),
        vmem((s, K * g.nlon, g.span * g.nlon), BF16), vmem((g.cells, K * C), BF16),
        vmem((g.cells, C), BF16), vmem((g.cells, H), BF16), vmem((g.cells, H), BF16),
        vmem((g.cells, C), BF16), vmem((g.cells, K * C), BF16),
        vmem((s + 2 * g.reach, g.nlon, C), F32),
        vmem((s, g.nlon, C), BF16), vmem((s, g.nlon, C), BF16),
        vmem((2, g.reach, g.nlon, C), BF16), vmem((2, g.reach, g.nlon, C), BF16),
        vmem((g.cores, half, rc, C), BF16), vmem((g.cores, half, rio, C), BF16),
        vmem((half, rc, C), BF16), vmem((half, rio, C), BF16),
        vmem((half, rc, C), BF16), vmem((half, rio, C), BF16),
        vmem((slots(g.rows), after_lat, rc, C), BF16),
        vmem((slots(g.members), after_ens, rio, C), BF16),
        vmem((after_lat, rc, C), BF16), vmem((after_ens, rio, C), BF16),
        vmem((slots(g.members), L, rc, C), BF16), vmem((slots(g.rows), L, rio, C), BF16),
        vmem((L, rc, C), BF16), vmem((L, rio, C), BF16),
        vmem((slots(L), rc, C), BF16), vmem((slots(L), rio, C), BF16),
        dma((7,)), dma((slots(L), 3)), dma((slots(L), 3)), dma((4,)),
        dma((slots(L),)), dma((slots(L),)), dma((slots(L),)), dma((slots(L),)),
        dma((slots(L),)), dma((slots(L),)), dma((2,)), dma((2,)),
        dma((2, cuts)), dma((2, cuts)), dma((4, cuts, peers)), dma((4, cuts, peers)),
        dma((2, cuts, slots(L))), dma((2, cuts, slots(L))),
    ]
    in_vmem = pl.BlockSpec(memory_space=pltpu.VMEM)
    anywhere = pl.BlockSpec(memory_space=pl.ANY)
    block_out, field_grad, conv_sum, io_sum = pl.pallas_call(
        functools.partial(kernel, g),
        out_shape=(
            jax.ShapeDtypeStruct(fields.shape, BF16),
            jax.ShapeDtypeStruct(fields.shape, BF16),
            jax.ShapeDtypeStruct((rc, C), F32),
            jax.ShapeDtypeStruct((rio, C), F32),
        ),
        in_specs=[anywhere] * 7,
        out_specs=(in_vmem,) * 4,
        scratch_shapes=scratch,
        compiler_params=pltpu.CompilerParams(
            collective_id=0, has_side_effects=True, vmem_limit_bytes=56 * 1024 * 1024),
        cost_estimate=pl.CostEstimate(
            flops=24 * g.cells * C * H, bytes_accessed=16 * C * H, transcendentals=2 * g.cells * H),
    )(filter_basis, lon_offsets.transpose(1, 0, 2), fields, cotangent, conv_weight, weight_in, weight_out)

    factor = 1.0 / math.sqrt(g.ens * g.lat * L * g.cells)
    rows = g.in_rows
    if g.members == g.ens:
        outs = pl.pallas_call(
            functools.partial(finish, rows, factor),
            out_shape=(
                jax.ShapeDtypeStruct(fields.shape, BF16),
                jax.ShapeDtypeStruct(fields.shape, BF16),
                jax.ShapeDtypeStruct((rc, C), F32),
                jax.ShapeDtypeStruct((rows, C), F32),
                jax.ShapeDtypeStruct((rows, C), F32),
            ),
            in_specs=[in_vmem] * 4,
            out_specs=(in_vmem,) * 5,
        )(block_out, field_grad, conv_sum, io_sum)
        return outs[:3] + (outs[3].T, outs[4])
    conv_sum, in_sum, out_sum = (
        lax.psum_scatter(part.astype(BF16), "ens", scatter_dimension=0, tiled=True).astype(F32)
        for part in (conv_sum, io_sum[:rows], io_sum[rows:])
    )
    return (block_out, field_grad, conv_sum * factor, in_sum.T * factor, out_sum * factor)


def solution(mesh):
    tiles = P("ens", "lat", "lon", None)
    bands = ("lat", "lon")
    blocks = ("lat", "lon", "ens")
    return jax.shard_map(
        shards,
        mesh=mesh,
        in_specs=(tiles, P(bands, None, None, None), P(bands, None, None), P(), P(), P(), tiles),
        out_specs=(tiles, tiles, P(blocks, None), P(None, blocks), P(blocks, None)),
        check_vma=False,
    )
```

profile of v0, /device:TPU:0, one launch (start us, length us, event | category | flops | bytes accessed | tf_op | source)
XLA Modules:
  0.0 78.4 jit_solution(12540724089343825907)
XLA Ops:
  0.6 75.6 %shard_map.110 = (bf16[1,12,16,640]{3,2,1,0:T(8,128)(2,1)}, bf16[1,12,16,640]{3,2,1,0:T(8,128)(2,1)}, f32[80,640]{1,0:T(8,128)}, f32[80,640]{1,0:T(8,128)}) custom-call(bf16[3,5,4,16]{3,2,1,0:T(4,128)(2,1)} %basis_hbm.1, s32[5,3,16]{2,1,0:T(4,128)} %bitcast.3, bf16[1,12,16,640]{3,2,1,0:T(8,128)(2,1)} %fields.1, bf16[1,12,16,640]{3,2,1,0:T(8,128)(2,1)} %cot.1, ...), custom_call_target="tpu_custom_call" | custom-call | flops 3774873600 | bytes 13107200 | tf_op jit(solution)/shard_map/pallas_call | solution.py:538
  76.2 2.2 %shard_map.111 = (bf16[1,12,16,640]{3,2,1,0:T(8,128)(2,1)}, bf16[1,12,16,640]{3,2,1,0:T(8,128)(2,1)}, f32[80,640]{1,0:T(8,128)}, f32[40,640]{1,0:T(8,128)}, f32[40,640]{1,0:T(8,128)}) custom-call(bf16[1,12,16,640]{3,2,1,0:T(8,128)(2,1)} %get-tuple-element.14.bo, bf16[1,12,16,640]{3,2,1,0:T(8,128)(2,1)} %get-tuple-element.15.fg, ...), custom_call_target="tpu_custom_call" | custom-call | tf_op jit(solution)/shard_map/pallas_call | solution.py:558
where the time goes:
time: 78.6 us; the launch traced here: 78.4 us
  Pallas kernels  77.8 us (99%)
    pallas_call x1, Pallas kernels, shards(): pl.pallas_call(functools.partial(kernel, g), out_shape=(jax.ShapeDtypeStr...  75.6 us
    pallas_call x1, Pallas kernels, shards(): pl.pallas_call(functools.partial(finish, rows, factor), out_shape=(jax.Sh...  2.2 us

commit v1 on v0

--- a/solution.py
+++ b/solution.py
@@ -51,7 +51,7 @@
 def kernel(
     g, basis_hbm, offsets_hbm, fields, cot, conv_hbm, in_hbm, out_hbm,
     block_out, field_grad, conv_out, io_out,
-    basis_ref, offsets_ref, taps_ref, conv_w, w_in, w_out, win, cot_band, matrix, spread, blended, hidden, pgrad, bgrad,
+    basis_ref, offsets_ref, taps_ref, conv_w, w_in, w_out, win, cot_band, matrix, spread, blended, hidden, slope, pgrad, bgrad,
     sgrad, adj, bo_band, fg_band, rim_send, rim_recv,
     conv_g, io_g, conv_c, io_c, conv_s0, io_s0, conv_r1, io_r1, conv_s1, io_s1,
     conv_r2, io_r2, conv_s2, io_s2, conv_r3, io_r3,
@@ -244,26 +244,37 @@
         win[rr:rr + s].reshape(g.cells, C).astype(F32) + mm(spread[...], conv_w[...], (1, 0))
     ).astype(BF16)
 
+    weights[1].wait()
+    weights[2].wait()
+    lanes = 256 if g.hidden % 256 == 0 else g.hidden
+
+    def unit_cols(i):
+        return pl.ds(pl.multiple_of(i * lanes, lanes), lanes)
+
+    def units(i, _):
+        cols = unit_cols(i)
+        pre = mm(blended[...], w_in[:, cols], (1, 0))
+        cdf = 0.5 * (1.0 + lax.erf(pre * HALF_ROOT))
+        hidden[:, cols] = (pre * cdf).astype(BF16)
+        slope[:, cols] = cdf + pre * jnp.exp(-0.5 * pre * pre) * GAUSS_NORM
+        return 0
+
+    def unit_grads(i, _):
+        cols = unit_cols(i)
+        hgrad = mm(cot_band[...].reshape(g.cells, C), w_out[cols, :], (1, 1))
+        pgrad[:, cols] = (hgrad * slope[:, cols]).astype(BF16)
+        return 0
+
+    lax.fori_loop(0, g.hidden // lanes, units, 0)
+    bo_band[...] = (
+        blended[...].astype(F32) + mm(hidden[...], w_out[...], (1, 0))
+    ).astype(BF16).reshape(s, NL, C)
     own_cot.wait()
     for d in range(1, L):
         source = lax.rem(j - d + L, L)
         landed = cot_band.at[:, columns(source)]
         remote(landed, landed, cot_send.at[d - 1], cot_recv.at[d - 1], lon=source).wait_recv()
-    weights[1].wait()
-    weights[2].wait()
-    lanes = 256 if g.hidden % 256 == 0 else g.hidden
-
-    def units(i, _):
-        cols = pl.ds(pl.multiple_of(i * lanes, lanes), lanes)
-        pre = mm(blended[...], w_in[:, cols], (1, 0))
-        cdf = 0.5 * (1.0 + lax.erf(pre * HALF_ROOT))
-        hidden[:, cols] = (pre * cdf).astype(BF16)
-        hgrad = mm(cot_band[...].reshape(g.cells, C), w_out[cols, :], (1, 1))
-        slope = cdf + pre * jnp.exp(-0.5 * pre * pre) * GAUSS_NORM
-        pgrad[:, cols] = (hgrad * slope).astype(BF16)
-        return 0
-
-    lax.fori_loop(0, g.hidden // lanes, units, 0)
+    lax.fori_loop(0, g.hidden // lanes, unit_grads, 0)
 
     def send_tiles(band, out, ssem, rsem):
         copies = []
@@ -302,23 +313,33 @@
             return blocks[0] + blocks[1]
         return sum((block.astype(F32) for block in blocks[1:]), blocks[0].astype(F32)).astype(BF16)
 
-    def io_blocks(i, _):
-        cols = pl.ds(pl.multiple_of(i * C, 128), C)
-        left = mm(pgrad[:, cols], blended[...], (0, 0))
-        right = mm(hidden[:, cols], cot_band[...].reshape(g.cells, C), (0, 0))
-        for c in range(C // ri):
-            where, flat = place(i * (C // ri) + c, "ens")
-            both = jnp.concatenate([left[c * ri:(c + 1) * ri], right[c * ri:(c + 1) * ri]], 0)
-            io_g[where, flat] = both.astype(BF16)
-        return 0
-
-    def conv_blocks(i, _):
-        cols = pl.ds(pl.multiple_of(i * C, 128), C)
-        product = mm(spread[:, cols], bgrad[...], (0, 0))
-        for c in range(C // rc):
-            where, flat = place(i * (C // rc) + c, "lat")
-            conv_g[where, flat] = product[c * rc:(c + 1) * rc].astype(BF16)
-        return 0
+    def io_blocks(h):
+        first, count = g.groups[h]
+
+        def one(i, _):
+            cols = pl.ds(pl.multiple_of(i * C, 128), C)
+            left = mm(pgrad[:, cols], blended[:, cut(h)], (0, 0))
+            tangent = cot_band[:, :, first:first + count].reshape(g.cells, count)
+            right = mm(hidden[:, cols], tangent, (0, 0))
+            for c in range(C // ri):
+                where, flat = place(i * (C // ri) + c, "ens")
+                both = jnp.concatenate(
+                    [left[c * ri:(c + 1) * ri], right[c * ri:(c + 1) * ri]], 0)
+                io_g[where, flat, :, cut(h)] = both.astype(BF16)
+            return 0
+
+        lax.fori_loop(0, g.hidden // C, one, 0)
+
+    def conv_blocks(h):
+        def one(i, _):
+            cols = pl.ds(pl.multiple_of(i * C, 128), C)
+            product = mm(spread[:, cols], bgrad[:, cut(h)], (0, 0))
+            for c in range(C // rc):
+                where, flat = place(i * (C // rc) + c, "lat")
+                conv_g[where, flat, :, cut(h)] = product[c * rc:(c + 1) * rc].astype(BF16)
+            return 0
+
+        lax.fori_loop(0, K, one, 0)
 
     def core_copies(src, dst, index):
         return [
@@ -382,43 +403,41 @@
             block = block + dst[d, :, cut(h)].astype(F32)
         total[:, cut(h)] = block
 
-    lax.fori_loop(0, g.hidden // C, io_blocks, 0)
     io_core = core_copies(io_g, io_c, 0)
     conv_core = core_copies(conv_g, conv_c, 1)
-    if g.cores > 1:
-        io_core[0].start()
-    bgrad[...] = (
-        cot_band[...].reshape(g.cells, C).astype(F32) + mm(pgrad[...], w_in[...], (1, 1))
-    ).astype(BF16)
     io_1, conv_1, io_2, conv_2, io_3, conv_3 = ([None for _ in groups] for _ in range(6))
+
+    def to_core(copies, h):
+        if g.cores > 1:
+            copies[h].start()
 
     def after_core(copies, total, own, other, h):
         if g.cores > 1:
             copies[h].wait()
         core_sum(total, own, other, h)
 
-    def start_rest(copies):
-        if g.cores > 1:
-            for copy in copies[1:]:
-                copy.start()
-
     def finish_stage(copies):
         for copy in copies:
             copy.wait()
 
-    start_rest(io_core)
+    io_blocks(0)
+    to_core(io_core, 0)
+    bgrad[...] = (
+        cot_band[...].reshape(g.cells, C).astype(F32) + mm(pgrad[...], w_in[...], (1, 1))
+    ).astype(BF16)
     after_core(io_core, io_s0, io_g, io_c, 0)
     io_1[0] = stage_start("ens", io_s0, io_r1, 0, 0)
-    lax.fori_loop(0, K, conv_blocks, 0)
-    if g.cores > 1:
-        conv_core[0].start()
-    bo_band[...] = (
-        blended[...].astype(F32) + mm(hidden[...], w_out[...], (1, 0))
-    ).astype(BF16).reshape(s, NL, C)
-    sends += send_tiles(bo_band, block_out, bo_send, bo_recv)
-    start_rest(conv_core)
+    conv_blocks(0)
+    to_core(conv_core, 0)
+    for h in groups[1:]:
+        io_blocks(h)
+        to_core(io_core, h)
     after_core(conv_core, conv_s0, conv_g, conv_c, 0)
     conv_1[0] = stage_start("lat", conv_s0, conv_r1, 0, 1)
+    sends += send_tiles(bo_band, block_out, bo_send, bo_recv)
+    for h in groups[1:]:
+        conv_blocks(h)
+        to_core(conv_core, h)
 
     sgrad[...] = mm(bgrad[...], conv_w[...], (1, 1)).astype(BF16)
     for r in range(s):
@@ -513,7 +532,8 @@
         vmem((s, (K + 1) * g.taps, g.span * g.nlon), F32), vmem((K * C, C), BF16), vmem((C, H), BF16), vmem((H, C), BF16),
         vmem((s + 2 * g.reach, g.nlon, C), BF16), vmem((s, g.nlon, C), BF16),
         vmem((s, K * g.nlon, g.span * g.nlon), BF16), vmem((g.cells, K * C), BF16),
-        vmem((g.cells, C), BF16), vmem((g.cells, H), BF16), vmem((g.cells, H), BF16),
+        vmem((g.cells, C), BF16), vmem((g.cells, H), BF16), vmem((g.cells, H), F32),
+        vmem((g.cells, H), BF16),
         vmem((g.cells, C), BF16), vmem((g.cells, K * C), BF16),
         vmem((s + 2 * g.reach, g.nlon, C), F32),
         vmem((s, g.nlon, C), BF16), vmem((s, g.nlon, C), BF16),

time: 78.6 us -> 78 us (level)
  no operation moved by 1% of the time
where the time goes in v1:
time: 78 us; the launch traced here: 77.8 us
  Pallas kernels  77.2 us (99%)
    pallas_call x1, Pallas kernels, shards(): pl.pallas_call(functools.partial(kernel, g), out_shape=(jax.ShapeDtypeStr...  75 us
    pallas_call x1, Pallas kernels, shards(): pl.pallas_call(functools.partial(finish, rows, factor), out_shape=(jax.Sh...  2.2 us

profile of v1, /device:TPU:0, one launch (start us, length us, event | category | flops | bytes accessed | tf_op | source)
XLA Modules:
  0.0 77.8 jit_solution(2042375627888330844)
XLA Ops:
  0.6 75.0 %shard_map.110 = (bf16[1,12,16,640]{3,2,1,0:T(8,128)(2,1)}, bf16[1,12,16,640]{3,2,1,0:T(8,128)(2,1)}, f32[80,640]{1,0:T(8,128)}, f32[80,640]{1,0:T(8,128)}) custom-call(bf16[3,5,4,16]{3,2,1,0:T(4,128)(2,1)} %basis_hbm.1, s32[5,3,16]{2,1,0:T(4,128)} %bitcast.3, bf16[1,12,16,640]{3,2,1,0:T(8,128)(2,1)} %fields.1, bf16[1,12,16,640]{3,2,1,0:T(8,128)(2,1)} %cot.1, ...), custom_call_target="tpu_custom_call" | custom-call | flops 3774873600 | bytes 13107200 | tf_op jit(solution)/shard_map/pallas_call | solution.py:558
  75.6 2.2 %shard_map.111 = (bf16[1,12,16,640]{3,2,1,0:T(8,128)(2,1)}, bf16[1,12,16,640]{3,2,1,0:T(8,128)(2,1)}, f32[80,640]{1,0:T(8,128)}, f32[40,640]{1,0:T(8,128)}, f32[40,640]{1,0:T(8,128)}) custom-call(bf16[1,12,16,640]{3,2,1,0:T(8,128)(2,1)} %get-tuple-element.14.bo, bf16[1,12,16,640]{3,2,1,0:T(8,128)(2,1)} %get-tuple-element.15.fg, ...), custom_call_target="tpu_custom_call" | custom-call | tf_op jit(solution)/shard_map/pallas_call | solution.py:578
